TPU v7x, 32 devices: a whole 2x2x4 slice. The times are simulated.
32 devices in a mesh: dp: 4 (over z), space: 8 (over y, x, core).
Axes of the slice: x: 2, y: 2, z: 4, core: 2. Of those that a mesh axis runs over, the one named last changes fastest.
Arguments:
- activations: bfloat16 [4, 16, 180, 768], P('dp', 'space'), may hold values from -6 to 6
- cotangent: bfloat16 [4, 16, 180, 768], P('dp', 'space'), may hold values from -6 to 6
- w_first: bfloat16 [2, 768, 96], replicated, may hold values from -0.4375 to 0.4375
- w_second: bfloat16 [2, 768, 96], replicated, may hold values from -0.4375 to 0.4375
- b_first: float32 [2, 768], replicated, may hold values from -3 to 3
- lon_keep: int32 [8], replicated, may hold values from 0 to 90, as said below
- relu_mask: int32 [4, 16, 2, 8, 768], P('dp', None, None, 'space'), may hold values 0 or 1
- shrink_mask: int32 [4, 16, 2, 8, 768], P('dp', None, None, 'space'), may hold values 0 or 1
Outputs:
- grad_activations: bfloat16 [4, 16, 180, 768], P('dp', 'space')
- grad_w_first: float32 [2, 768, 96], P(None, 'dp')
- grad_w_second: float32 [2, 768, 96], P(None, 'dp')
- grad_b_first: float32 [2, 768], P(None, 'dp')
- grad_b_second: float32 [2, 768], P(None, 'dp')
Inputs may be any that keep to these rules, and one draw needn't show every extreme that they name: `lon_keep`: 8 distinct longitude frequencies, 0 and 90 among them, in no particular order.
All inputs are finite; a program needn't handle non-finite values. No bound on the sum of `relu_mask` or of `shrink_mask` on one device may be relied on, other than what follows from the above.
Results may differ from a plain program's by a relative error of at most 0.011.
Values may be sent and summed in bfloat16 or wider, within the bound.
No kernel may reach another device: no remote copies, remote signals or barrier semaphores. Data moves between devices by JAX's collectives and lax.ppermute only.
A program may use at most 64 MiB of HBM per device.

v0:
```python
import functools
import math

import jax
import jax.numpy as jnp
import numpy as np
from jax import lax
from jax.experimental import pallas as pl
from jax.experimental.pallas import tpu as pltpu
from jax.sharding import PartitionSpec as P

C = 768
BLOCKS = 8
LON = 180
BS = 96

BF = jnp.bfloat16
F32 = jnp.float32
LANES = 128
THIRD = LANES - BS
VMEM_LIMIT = 32 * 1024 * 1024
WHOLE_VMEM = 60 * 1024 * 1024


def shift_of(group):
    return 2 * (group % 2) + group // 2


def block_of(group, device):
    lane = 2 * (device // 4) + device % 2
    return 2 * ((lane + shift_of(group)) % 4) + (device // 2) % 2


def owner_of(group, block):
    lane = (block // 2 + 4 - shift_of(group)) % 4
    return 4 * (lane // 2) + 2 * (block % 2) + lane % 2


def latitude_matrix(lat_len, kept):
    index = np.arange(lat_len)
    angle = ((index[:, None] * index[None, :]) % lat_len).astype(np.float32) * np.float32(
        2.0 * math.pi / lat_len
    )
    cosine, sine = np.cos(angle), np.sin(angle)
    table = np.stack([np.stack([cosine, sine], -1), np.stack([-sine, cosine], -1)], 1)
    full = np.einsum("mphq,jk->pjmhqk", table, np.eye(kept, dtype=np.float32))
    return full.reshape(2 * kept * lat_len, 2 * kept * lat_len)


def dot(lhs, rhs, lhs_axis, rhs_axis):
    return lax.dot_general(
        lhs, rhs, (((lhs_axis,), (rhs_axis,)), ((), ())), preferred_element_type=F32
    )


def fold(array):
    rows = array.shape[0] // 4
    beside = [array[3 * rows :, g * THIRD : (g + 1) * THIRD] for g in range(3)]
    return jnp.concatenate([array[: 3 * rows], jnp.concatenate(beside, axis=0)], axis=1)


def unfold(array):
    rows = array.shape[0] // 3
    beside = [array[g * rows : (g + 1) * rows, BS:] for g in range(3)]
    return jnp.concatenate([array[:, :BS], jnp.concatenate(beside, axis=1)], axis=0)


def forward_lon_kernel(
    keep_hbm, act_hbm, cot_hbm, relu_hbm, shrink_hbm, out, table_out, field, masks, keep, sems
):
    kept = keep.shape[0]
    rows = act_hbm.shape[1]
    modes = relu_hbm.shape[0]
    tiles = C // LANES
    columns = [slice(k * LANES, (k + 1) * LANES) for k in range(tiles)]
    keep_copy = pltpu.make_async_copy(keep_hbm, keep, sems.at[0])
    keep_copy.start()
    field_copies, mask_copies = [], []
    for t, source in enumerate((act_hbm, cot_hbm)):
        for k in range(tiles):
            copy = pltpu.make_async_copy(
                source.at[:, :, columns[k]], field.at[t, k], sems.at[1 + t * tiles + k]
            )
            copy.start()
            field_copies.append(copy)
    for t, source in enumerate((relu_hbm, shrink_hbm)):
        for p in range(2):
            for k in range(tiles):
                copy = pltpu.make_async_copy(
                    source.at[:, p, :, columns[k]],
                    masks.at[t, p, k],
                    sems.at[1 + (2 + 2 * t + p) * tiles + k],
                )
                copy.start()
                mask_copies.append(copy)

    keep_copy.wait()
    shape = (rows * 2 * kept, LON * rows)
    line = lax.broadcasted_iota(jnp.int32, shape, 0)
    column = lax.broadcasted_iota(jnp.int32, shape, 1)
    frequency = jnp.zeros(shape, jnp.int32)
    for j in range(kept):
        frequency = jnp.where(line % kept == j, keep[j], frequency)
    turn = jnp.where((line // kept) % 2 == 1, LON // 4, 0)
    phase = ((column // rows) * frequency + turn) % LON
    table = jnp.cos(phase.astype(F32) * (2.0 * math.pi / LON))
    table = jnp.where(line // (2 * kept) == column % rows, table, 0.0).astype(BF)
    table_out[...] = table

    group = lax.axis_index("dp")
    own = keep[lax.axis_index("space")]
    scale = jnp.where((own == 0) | (2 * own == LON), 1.0, 2.0)
    for copy in mask_copies:
        copy.wait()

    def gate(t, value):
        return jnp.concatenate(
            [
                jnp.concatenate(
                    [
                        jnp.where(masks.at[t, p, k].reshape(modes, LANES)[...] > 0, value, 0.0)
                        for k in range(tiles)
                    ],
                    axis=1,
                )
                for p in range(2)
            ],
            axis=0,
        ).astype(BF)

    passed = gate(0, 1.0)
    scaled = gate(1, scale)

    lines = []
    for t in range(2):
        found = []
        for k in range(0, tiles, 2):
            for i in range(2):
                field_copies[t * tiles + k + i].wait()
            wide = jnp.concatenate(
                [field.at[t, k + i].reshape(LON * rows, LANES)[...] for i in range(2)], axis=1
            )
            found.append(dot(table, wide, 1, 0).astype(BF))
        lines.append(jnp.concatenate(found, axis=1))

    packed = jnp.concatenate(lines + [passed, scaled], axis=0)
    for b in range(BLOCKS):
        out[owner_of(group, b)] = fold(packed[:, b * BS : (b + 1) * BS])


def spectral_kernel(
    pieces, first_all, second_all, bias, lat, lat_t, grad_lat, terms, *, ortho_scale, rows, kept
):
    device = lax.axis_index("space")
    block = block_of(lax.axis_index("dp"), device)
    parts = pieces.shape[0]
    per = rows * 2 * kept
    half = parts * per // 2
    modes = half // kept
    place = pl.ds(pl.multiple_of(block * BS, BS), BS)
    first = [first_all[p, place, :] for p in range(2)]
    second = [second_all[p, place, :] for p in range(2)]
    opened = [unfold(pieces[i]) for i in range(parts)]

    def spectrum(t):
        stacked = jnp.concatenate([piece[t * per : (t + 1) * per] for piece in opened], axis=0)
        return (dot(lat[...], stacked, 1, 0) * ortho_scale).astype(BF)

    def mask(k):
        start = 2 * per + k * 2 * modes
        return jnp.concatenate(
            [
                opened[j][start + p * modes : start + (p + 1) * modes]
                for p in range(2)
                for j in range(kept)
            ],
            axis=0,
        ).astype(F32)

    spec_act = spectrum(0)
    spec_cot = spectrum(1)
    passed = mask(0) > 0.0
    weight = mask(1)
    grad_out = jnp.where(weight > 0.0, weight * spec_cot.astype(F32), 0.0).astype(BF)

    bias_real = jnp.zeros((1, BS), F32)
    bias_imag = jnp.zeros((1, BS), F32)
    for b in range(BLOCKS):
        mine = block == b
        bias_real = jnp.where(mine, bias[0:1, b * BS : (b + 1) * BS], bias_real)
        bias_imag = jnp.where(mine, bias[1:2, b * BS : (b + 1) * BS], bias_imag)

    by_real = dot(spec_act, first[0], 1, 0)
    by_imag = dot(spec_act, first[1], 1, 0)
    pre = jnp.concatenate(
        [
            by_real[:half] - by_imag[half:] + bias_real,
            by_imag[:half] + by_real[half:] + bias_imag,
        ],
        axis=0,
    )
    hidden = jnp.where(passed, pre, 0.0).astype(BF)

    def adjoint(operand, matrix):
        real = dot(operand, matrix[0], 1, 1)
        imag = dot(operand, matrix[1], 1, 1)
        return jnp.concatenate([real[:half] + imag[half:], real[half:] - imag[:half]], axis=0)

    grad_pre = jnp.where(passed, adjoint(grad_out, second), 0.0).astype(BF)

    def turned(array):
        return jnp.concatenate([array[half:], -array[:half]], axis=0)

    at = 2 * BS * 3 // 4
    for a, (left, right) in enumerate(((spec_act, grad_pre), (hidden, grad_out))):
        slot = (a + device) % 2
        matrices = jnp.concatenate(
            [dot(left, right, 0, 0), dot(left, turned(right), 0, 0)], axis=0
        )
        terms[slot, 0:at, :] = fold(matrices).astype(BF)
        wide = right.astype(F32)
        sums = [jnp.sum(wide[p * half : (p + 1) * half], axis=0, keepdims=True) for p in range(2)]
        rest = terms.shape[1] - at
        sums = jnp.concatenate(sums + [jnp.zeros((rest - 2, BS), F32)], axis=0)
        terms[slot, at:, :] = jnp.concatenate(
            [sums, jnp.zeros((rest, THIRD), F32)], axis=1
        ).astype(BF)

    grad_spec = adjoint(grad_pre, first).astype(BF)
    lines = dot(lat_t[...], grad_spec, 1, 0)
    lines = jnp.concatenate([lines, jnp.zeros((2 * half, THIRD), F32)], axis=1).astype(BF)
    grad_lat[...] = lines.reshape(grad_lat.shape)


def inverse_lon_kernel(
    table,
    pieces,
    field_hbm,
    first_hbm,
    second_hbm,
    bias_first,
    bias_second,
    lines,
    field,
    matrices,
    sems,
    *,
    ortho_scale,
    grad_norm,
):
    rows = field_hbm.shape[1]
    per = table.shape[0]
    tiles = C // LANES
    group = lax.axis_index("dp")
    matrix_rows = 2 * BS * 3 // 4
    copies = []
    for b in range(BLOCKS):
        lines[:, b * BS : (b + 1) * BS] = pieces[owner_of(group, b), 0:per, 0:BS]
    for k in range(0, tiles, 2):
        wide = dot(table[...], lines[:, k * LANES : (k + 2) * LANES], 0, 0) * ortho_scale
        for i in range(2):
            field.at[k + i].reshape(LON * rows, LANES)[...] = wide[
                :, i * LANES : (i + 1) * LANES
            ].astype(BF)
            copy = pltpu.make_async_copy(
                field.at[k + i],
                field_hbm.at[:, :, (k + i) * LANES : (k + i + 1) * LANES],
                sems.at[k + i],
            )
            copy.start()
            copies.append(copy)
    for a, (target, vector) in enumerate(((first_hbm, bias_first), (second_hbm, bias_second))):
        for k in range(2):
            sources = [pieces[4 * y + 2 * k + a, per:, :].astype(F32) for y in range(2)]
            total = (sources[0] + sources[1]) * grad_norm
            opened = unfold(total[:matrix_rows])
            for p in range(2):
                matrices[a, p, k * BS : (k + 1) * BS, :] = opened[p * BS : (p + 1) * BS]
                vector[p : p + 1, k * BS : (k + 1) * BS] = total[
                    matrix_rows + p : matrix_rows + p + 1, :BS
                ]
        copy = pltpu.make_async_copy(matrices.at[a], target, sems.at[tiles + a])
        copy.start()
        copies.append(copy)
    for copy in copies:
        copy.wait()


def whole(memory=pltpu.VMEM):
    return pl.BlockSpec(memory_space=memory)


def by_blocks(
    activations, cotangent, w_first, w_second, b_first, lon_keep, relu_mask, shrink_mask
):
    groups = lax.axis_size("dp")
    parts = lax.axis_size("space")
    rows = activations.shape[1]
    lat_len = rows * parts
    kept = lon_keep.shape[0]
    ortho_scale = 1.0 / math.sqrt(lat_len * LON)
    grad_norm = 1.0 / math.sqrt(groups * lat_len * kept)
    params = pltpu.CompilerParams(vmem_limit_bytes=VMEM_LIMIT)
    tiles = C // LANES
    per = rows * 2 * kept
    height = (2 * per + 4 * lat_len) * 3 // 4
    term_rows = 2 * BS * 3 // 4 + 16

    sent, table = pl.pallas_call(
        forward_lon_kernel,
        out_shape=(
            jax.ShapeDtypeStruct((parts, height, LANES), BF),
            jax.ShapeDtypeStruct((per, LON * rows), BF),
        ),
        in_specs=[whole(pl.ANY)] * 5,
        out_specs=(whole(), whole()),
        scratch_shapes=[
            pltpu.VMEM((2, tiles, LON, rows, LANES), BF),
            pltpu.VMEM((2, 2, tiles, lat_len, 1, LANES), jnp.int32),
            pltpu.SMEM((kept,), jnp.int32),
            pltpu.SemaphoreType.DMA((1 + 6 * tiles,)),
        ],
        compiler_params=pltpu.CompilerParams(vmem_limit_bytes=WHOLE_VMEM),
        name="forward_lon",
    )(
        lon_keep,
        activations[0].transpose(1, 0, 2),
        cotangent[0].transpose(1, 0, 2),
        relu_mask[0],
        shrink_mask[0],
    )
    pieces = lax.all_to_all(sent, "space", 0, 0, tiled=True)

    lat = latitude_matrix(lat_len, kept)
    grad_lat, terms = pl.pallas_call(
        functools.partial(spectral_kernel, ortho_scale=ortho_scale, rows=rows, kept=kept),
        out_shape=(
            jax.ShapeDtypeStruct((parts, per, LANES), BF),
            jax.ShapeDtypeStruct((2, term_rows, LANES), BF),
        ),
        in_specs=[whole()] * 6,
        out_specs=(whole(), whole()),
        compiler_params=params,
        name="spectral",
    )(pieces, w_first, w_second, b_first, jnp.asarray(lat, BF), jnp.asarray(lat.T, BF))

    arrived = lax.ppermute(
        terms,
        ("dp", "space"),
        [
            (g * parts + c, (block_of(g, c) // 2) * parts + c)
            for g in range(groups)
            for c in range(parts)
        ],
    )
    other = lax.ppermute(arrived[1], "space", [(c, c ^ 1) for c in range(parts)])
    share = (arrived[0].astype(F32) + other.astype(F32)).astype(BF)
    returned = lax.all_to_all(
        jnp.concatenate(
            [grad_lat, jnp.broadcast_to(share[None], (parts,) + share.shape)], axis=1
        ),
        "space",
        0,
        0,
        tiled=True,
    )

    keep_rows = C // groups
    field, first, second, bias_first, bias_second = pl.pallas_call(
        functools.partial(inverse_lon_kernel, ortho_scale=ortho_scale, grad_norm=grad_norm),
        out_shape=(
            jax.ShapeDtypeStruct((LON, rows, C), BF),
            jax.ShapeDtypeStruct((2, keep_rows, BS), F32),
            jax.ShapeDtypeStruct((2, keep_rows, BS), F32),
            jax.ShapeDtypeStruct((2, keep_rows), F32),
            jax.ShapeDtypeStruct((2, keep_rows), F32),
        ),
        in_specs=[whole(), whole()],
        out_specs=(whole(pl.ANY),) * 3 + (whole(),) * 2,
        scratch_shapes=[
            pltpu.VMEM((per, C), BF),
            pltpu.VMEM((tiles, LON, rows, LANES), BF),
            pltpu.VMEM((2, 2, keep_rows, BS), F32),
            pltpu.SemaphoreType.DMA((tiles + 2,)),
        ],
        compiler_params=params,
        name="inverse_lon",
    )(table, returned)
    return field.transpose(1, 0, 2)[None], first, second, bias_first, bias_second


def build_tables(lon_keep, lat_len, lon_len):
    columns = jnp.arange(lon_len, dtype=jnp.int32)
    lon_phase = columns[:, None] * lon_keep[None, :] % lon_len
    lon_angle = lon_phase.astype(jnp.float32) * (2.0 * math.pi / lon_len)
    lon_table = jnp.stack([jnp.cos(lon_angle), -jnp.sin(lon_angle)], axis=1).astype(jnp.bfloat16)
    latitudes = jnp.arange(lat_len, dtype=jnp.int32)
    lat_phase = latitudes[:, None] * latitudes[None, :] % lat_len
    lat_angle = lat_phase.astype(jnp.float32) * (2.0 * math.pi / lat_len)
    cosine = jnp.cos(lat_angle)
    sine_part = jnp.sin(lat_angle)
    lat_table = jnp.stack(
        [jnp.stack([cosine, sine_part], axis=-1), jnp.stack([-sine_part, cosine], axis=-1)], axis=1
    ).astype(jnp.bfloat16)
    return (lon_table, lat_table)


def apply_blocks(operand, matrix):
    return jnp.einsum("smjbc,bcd->smjbd", operand, matrix, preferred_element_type=jnp.float32)


def adjoint(operand, matrix):
    return jnp.einsum("smjbd,bcd->smjbc", operand, matrix, preferred_element_type=jnp.float32)


def outer_sum(operand, other):
    return jnp.einsum("smjbc,smjbd->bcd", operand, other, preferred_element_type=jnp.float32)


def by_frequencies(
    activations, cotangent, w_first, w_second, b_first, lon_keep, relu_mask, shrink_mask
):
    parts = lax.axis_size("space")
    samples_dev = activations.shape[0]
    lat_len = activations.shape[1] * parts
    kept = lon_keep.shape[0]
    owned = kept // parts
    lon_table, lat_table = build_tables(lon_keep, lat_len, LON)
    ortho_scale = 1.0 / math.sqrt(lat_len * LON)
    act_lon = jnp.einsum(
        "shwc,wpk->shpkc", activations, lon_table, preferred_element_type=jnp.float32
    ).astype(jnp.bfloat16)
    cot_lon = jnp.einsum(
        "shwc,wpk->shpkc", cotangent, lon_table, preferred_element_type=jnp.float32
    ).astype(jnp.bfloat16)
    act_modes, cot_modes = (
        lax.all_to_all(act_lon, "space", split_axis=3, concat_axis=1, tiled=True),
        lax.all_to_all(cot_lon, "space", split_axis=3, concat_axis=1, tiled=True),
    )

    def latitude(modes):
        summed = jnp.einsum(
            "mphq,shqjc->smpjc", lat_table, modes, preferred_element_type=jnp.float32
        )
        return (summed * ortho_scale).astype(jnp.bfloat16)

    block_shape = (samples_dev, lat_len, 2, owned, BLOCKS, BS)
    spec_act = latitude(act_modes).reshape(block_shape)
    spec_cot = latitude(cot_modes)
    own_keep = lax.dynamic_slice_in_dim(lon_keep, lax.axis_index("space") * owned, owned)
    doubled = jnp.where((own_keep == 0) | (2 * own_keep == LON), 1.0, 2.0).astype(jnp.float32)
    grad_out = (
        jnp.where(
            shrink_mask > 0, doubled[None, None, None, :, None] * spec_cot.astype(jnp.float32), 0.0
        )
        .astype(jnp.bfloat16)
        .reshape(block_shape)
    )
    relu_gate = relu_mask.reshape(block_shape) > 0
    first_blocks = w_first.reshape(2, BLOCKS, BS, BS)
    second_blocks = w_second.reshape(2, BLOCKS, BS, BS)
    bias_blocks = b_first.reshape(2, BLOCKS, BS)
    act_real = spec_act[:, :, 0]
    act_imag = spec_act[:, :, 1]
    pre_real = (
        apply_blocks(act_real, first_blocks[0])
        - apply_blocks(act_imag, first_blocks[1])
        + bias_blocks[0]
    )
    pre_imag = (
        apply_blocks(act_real, first_blocks[1])
        + apply_blocks(act_imag, first_blocks[0])
        + bias_blocks[1]
    )
    hidden = jnp.where(relu_gate, jnp.stack([pre_real, pre_imag], axis=2), 0.0).astype(jnp.bfloat16)
    out_real = grad_out[:, :, 0]
    out_imag = grad_out[:, :, 1]
    hidden_real = adjoint(out_real, second_blocks[0]) + adjoint(out_imag, second_blocks[1])
    hidden_imag = -adjoint(out_real, second_blocks[1]) + adjoint(out_imag, second_blocks[0])
    grad_pre = jnp.where(relu_gate, jnp.stack([hidden_real, hidden_imag], axis=2), 0.0).astype(
        jnp.bfloat16
    )
    pre_grad_real = grad_pre[:, :, 0]
    pre_grad_imag = grad_pre[:, :, 1]
    spec_real = adjoint(pre_grad_real, first_blocks[0]) + adjoint(pre_grad_imag, first_blocks[1])
    spec_imag = -adjoint(pre_grad_real, first_blocks[1]) + adjoint(pre_grad_imag, first_blocks[0])
    grad_spec = (
        jnp.stack([spec_real, spec_imag], axis=2)
        .astype(jnp.bfloat16)
        .reshape(samples_dev, lat_len, 2, owned, C)
    )
    first_grad = jnp.stack(
        [
            outer_sum(act_real, pre_grad_real) + outer_sum(act_imag, pre_grad_imag),
            outer_sum(act_real, pre_grad_imag) - outer_sum(act_imag, pre_grad_real),
        ]
    ).reshape(2, C, BS)
    hid_real = hidden[:, :, 0]
    hid_imag = hidden[:, :, 1]
    second_grad = jnp.stack(
        [
            outer_sum(hid_real, out_real) + outer_sum(hid_imag, out_imag),
            outer_sum(hid_real, out_imag) - outer_sum(hid_imag, out_real),
        ]
    ).reshape(2, C, BS)
    bias_first = jnp.sum(grad_pre, axis=(0, 1, 3), dtype=jnp.float32).reshape(2, C)
    bias_second = jnp.sum(grad_out, axis=(0, 1, 3), dtype=jnp.float32).reshape(2, C)
    local_terms = (first_grad, second_grad, bias_first, bias_second)
    summed = lax.psum(
        (local_terms[0], local_terms[1], local_terms[2], local_terms[3]), ("dp", "space")
    )
    share_rows = C // lax.axis_size("dp")
    row_start = lax.axis_index("dp") * share_rows

    def take_share(array):
        return lax.dynamic_slice_in_dim(array, row_start, share_rows, 1)

    totals = jax.tree.map(take_share, summed)
    grad_norm = 1.0 / math.sqrt(samples_dev * lax.axis_size("dp") * lat_len * kept)
    grad_lat = jnp.einsum(
        "mqhp,smqjc->shpjc", lat_table, grad_spec, preferred_element_type=jnp.float32
    ).astype(jnp.bfloat16)
    returned = lax.all_to_all(grad_lat, "space", split_axis=1, concat_axis=3, tiled=True)
    grad_field = (
        jnp.einsum("wpk,shpkc->shwc", lon_table, returned, preferred_element_type=jnp.float32)
        * ortho_scale
    ).astype(jnp.bfloat16)
    return (
        grad_field,
        totals[0] * grad_norm,
        totals[1] * grad_norm,
        totals[2] * grad_norm,
        totals[3] * grad_norm,
    )


def solution(mesh):
    groups, parts = mesh.shape["dp"], mesh.shape["space"]

    def per_device(*arrays):
        activations, lon_keep = arrays[0], arrays[5]
        fits = (
            parts == BLOCKS
            and 2 * groups == BLOCKS
            and activations.shape[:2] == (1, 2)
            and lon_keep.shape[0] == parts
        )
        return by_blocks(*arrays) if fits else by_frequencies(*arrays)

    return jax.shard_map(
        per_device,
        mesh=mesh,
        in_specs=(
            P("dp", "space", None, None),
            P("dp", "space", None, None),
            P(),
            P(),
            P(),
            P(),
            P("dp", None, None, "space", None),
            P("dp", None, None, "space", None),
        ),
        out_specs=(
            P("dp", "space", None, None),
            P(None, "dp", None),
            P(None, "dp", None),
            P(None, "dp"),
            P(None, "dp"),
        ),
        check_vma=False,
    )
```

profile of v0, /device:TPU:0, one launch (start us, length us, event | category | flops | bytes accessed | tf_op | source)
XLA Modules:
  0.0 37.5 jit_solution(9988036446399625543)
XLA Ops:
  0.6 3.6 %forward_lon.1 = (bf16[8,96,128]{2,1,0:T(8,128)(2,1)}, bf16[32,360]{1,0:T(8,128)(2,1)}) custom-call(s32[8]{0:T(128)} %keep_hbm.1, bf16[180,2,768]{2,1,0:T(2,128)(2,1)} %bitcast.18, bf16[180,2,768]{2,1,0:T(2,128)(2,1)} %bitcast.19, s32[16,2,1,768]{3,2,1,0:T(1,128)} %bitcast.20, s32[16,2,1,768]{3,2,1,0:T(1,128)} %bitcast.21), custom_call_target="tpu_custom_call" | custom-call | tf_op jit(solution)/shard_map/forward_lon/pallas_call | solution.py:309
  4.2 0.0 copy-start.4
  4.2 5.3 %all-to-all-start = ((bf16[8,96,128]{2,1,0:T(8,128)(2,1)}), bf16[8,96,128]{2,1,0:T(8,128)(2,1)S(1)}, u32[]{:S(2)}, u32[]{:S(2)}) async-start(bf16[8,96,128]{2,1,0:T(8,128)(2,1)} %get-tuple-element.15), calls=%async_computation | async-start | bytes 393216 | tf_op jit(solution)/shard_map/all_to_all | solution.py:332
  9.5 0.0 copy-done.4
  9.5 0.0 copy-start.5
  9.6 0.2 copy.15.first_all
  9.8 0.7 %copy-done.5 = bf16[2,768,96]{1,2,0:T(8,128)(2,1)S(1)} copy-done((bf16[2,768,96]{1,2,0:T(8,128)(2,1)S(1)}, bf16[2,768,96]{1,2,0:T(8,128)(2,1)}, u32[]{:S(2)}) %copy-start.5) | copy-done | bytes 294936
  10.5 0.0 copy-start
  10.5 0.0 copy-start.1
  10.5 0.0 copy-start.3
  10.5 0.2 copy.16.second_all
  10.7 5.0 %all-to-all-done.pieces = bf16[8,96,128]{2,1,0:T(8,128)(2,1)S(1)} async-done(((bf16[8,96,128]{2,1,0:T(8,128)(2,1)}), bf16[8,96,128]{2,1,0:T(8,128)(2,1)S(1)}, u32[]{:S(2)}, u32[]{:S(2)}) %all-to-all-start) | async-done | bytes 196640 | tf_op jit(solution)/shard_map/all_to_all | solution.py:332
  15.8 0.0 copy-done
  15.8 0.0 copy-done.1
  15.8 0.0 copy-done.3
  15.8 1.1 %spectral.1 = (bf16[8,32,128]{2,1,0:T(8,128)(2,1)S(1)}, bf16[2,160,128]{2,1,0:T(8,128)(2,1)S(1)}) custom-call(bf16[8,96,128]{2,1,0:T(8,128)(2,1)S(1)} %all-to-all-done.pieces, bf16[2,768,96]{2,1,0:T(8,128)(2,1)S(1)} %copy.15.first_all, bf16[2,768,96]{2,1,0:T(8,128)(2,1)S(1)} %copy.16.second_all, f32[2,768]{1,0:T(2,128)S(1)} %copy-done.3, ...), custom_call_target="tpu_custom_call" | custom-call | tf_op jit(solution)/shard_map/spectral/pallas_call | solution.py:335
  16.9 0.7 %collective-permute-start = (bf16[2,160,128]{2,1,0:T(8,128)(2,1)S(1)}, bf16[2,160,128]{2,1,0:T(8,128)(2,1)S(1)}, u32[]{:S(2)}, u32[]{:S(2)}) collective-permute-start(bf16[2,160,128]{2,1,0:T(8,128)(2,1)S(1)} %get-tuple-element.17), channel_id=1, source_target_pairs={{0,0},{1,9},{2,2},{3,11},{4,20},{5,29},{6,22},{7,31},{8,16},{9,25}... | collective-permute-start | bytes 245768 | tf_op jit(solution)/shard_map/ppermute | solution.py:347
  17.5 0.0 collective-permute-done
  17.6 5.9 %collective-permute-start.1 = (bf16[160,128]{1,0:T(8,128)(2,1)S(1)}, bf16[160,128]{1,0:T(8,128)(2,1)S(1)}, u32[]{:S(2)}, u32[]{:S(2)}) collective-permute-start(bf16[160,128]{1,0:T(8,128)(2,1)S(1)} %slice_bitcast_fusion), channel_id=1, source_target_pairs={{0,1},{1,0},{2,3},{3,2},{4,5},{5,4},{6,7},{7,6},{8,9},{9,8},{10,11... | collective-permute-start | bytes 122888 | tf_op jit(solution)/shard_map/ppermute | solution.py:356
  23.5 0.9 %collective-permute-done.1 = bf16[160,128]{1,0:T(8,128)(2,1)S(1)} collective-permute-done((bf16[160,128]{1,0:T(8,128)(2,1)S(1)}, bf16[160,128]{1,0:T(8,128)(2,1)S(1)}, u32[]{:S(2)}, u32[]{:S(2)}) %collective-permute-start.1) | collective-permute-done | bytes 40992 | tf_op jit(solution)/shard_map/ppermute | solution.py:356
  24.5 0.0 copy-start.2
  24.5 10.8 %all_to_all.10.pieces = bf16[8,192,128]{2,1,0:T(8,128)(2,1)S(1)} all-to-all(bf16[8,192,128]{2,1,0:T(8,128)(2,1)S(1)} %pad_maximum_fusion), channel_id=1, replica_groups=mesh['dp'=4,'space'=8] {'space'}, dimensions={0} | all-to-all | bytes 786432 | tf_op jit(solution)/shard_map/all_to_all | solution.py:358
  35.3 0.0 copy-done.2
  35.3 2.2 %inverse_lon.1 = (bf16[180,2,768]{2,1,0:T(2,128)(2,1)}, f32[2,192,96]{2,1,0:T(8,128)}, f32[2,192,96]{2,1,0:T(8,128)}, f32[2,192]{1,0:T(2,128)}, f32[2,192]{1,0:T(2,128)}) custom-call(bf16[32,360]{1,0:T(8,128)(2,1)S(1)} %copy-done.2, bf16[8,192,128]{2,1,0:T(8,128)(2,1)S(1)} %all_to_all.10.pieces), custom_call_target="tpu_custom_call" | custom-call | tf_op jit(solution)/shard_map/inverse_lon/pallas_call | solution.py:369
  (4 shorter events, 0.1 us)
Async XLA Ops:
  4.2 5.3 %copy-start.4 = (bf16[2,768,96]{1,2,0:T(8,128)(2,1)S(1)}, bf16[2,768,96]{1,2,0:T(8,128)(2,1)}, u32[]{:S(2)}) copy-start(bf16[2,768,96]{1,2,0:T(8,128)(2,1)} %param.12) | copy-start | bytes 884740
  4.2 11.5 %all-to-all-start = ((bf16[8,96,128]{2,1,0:T(8,128)(2,1)}), bf16[8,96,128]{2,1,0:T(8,128)(2,1)S(1)}, u32[]{:S(2)}, u32[]{:S(2)}) async-start(bf16[8,96,128]{2,1,0:T(8,128)(2,1)} %get-tuple-element.15), calls=%async_computation | async-start | bytes 393216 | tf_op jit(solution)/shard_map/all_to_all | solution.py:332
  9.5 1.0 %copy-start.5 = (bf16[2,768,96]{1,2,0:T(8,128)(2,1)S(1)}, bf16[2,768,96]{1,2,0:T(8,128)(2,1)}, u32[]{:S(2)}) copy-start(bf16[2,768,96]{1,2,0:T(8,128)(2,1)} %param.13) | copy-start | bytes 884740
  10.5 5.3 %copy-start = (bf16[256,256]{1,0:T(8,128)(2,1)S(1)}, bf16[256,256]{1,0:T(8,128)(2,1)}, u32[]{:S(2)}) copy-start(bf16[256,256]{1,0:T(8,128)(2,1)} %constant.5.clone.lat_t) | copy-start | bytes 393220
  10.5 5.3 %copy-start.1 = (bf16[256,256]{1,0:T(8,128)(2,1)S(1)}, bf16[256,256]{1,0:T(8,128)(2,1)}, u32[]{:S(2)}) copy-start(bf16[256,256]{1,0:T(8,128)(2,1)} %constant.4.clone.lat) | copy-start | bytes 393220
  10.5 5.3 %copy-start.3 = (f32[2,768]{1,0:T(2,128)S(1)}, f32[2,768]{1,0:T(2,128)}, u32[]{:S(2)}) copy-start(f32[2,768]{1,0:T(2,128)} %bias.1) | copy-start | bytes 18436
  16.9 0.7 %collective-permute-start = (bf16[2,160,128]{2,1,0:T(8,128)(2,1)S(1)}, bf16[2,160,128]{2,1,0:T(8,128)(2,1)S(1)}, u32[]{:S(2)}, u32[]{:S(2)}) collective-permute-start(bf16[2,160,128]{2,1,0:T(8,128)(2,1)S(1)} %get-tuple-element.17), channel_id=1, source_target_pairs={{0,0},{1,9},{2,2},{3,11},{4,20},{5,29},{6,22},{7,31},{8,16},{9,25}... | collective-permute-start | bytes 245768 | tf_op jit(solution)/shard_map/ppermute | solution.py:347
  17.6 6.8 %collective-permute-start.1 = (bf16[160,128]{1,0:T(8,128)(2,1)S(1)}, bf16[160,128]{1,0:T(8,128)(2,1)S(1)}, u32[]{:S(2)}, u32[]{:S(2)}) collective-permute-start(bf16[160,128]{1,0:T(8,128)(2,1)S(1)} %slice_bitcast_fusion), channel_id=1, source_target_pairs={{0,1},{1,0},{2,3},{3,2},{4,5},{5,4},{6,7},{7,6},{8,9},{9,8},{10,11... | collective-permute-start | bytes 122888 | tf_op jit(solution)/shard_map/ppermute | solution.py:356
  24.5 10.8 %copy-start.2 = (bf16[32,360]{1,0:T(8,128)(2,1)S(1)}, bf16[32,360]{1,0:T(8,128)(2,1)}, u32[]{:S(2)}) copy-start(bf16[32,360]{1,0:T(8,128)(2,1)} %get-tuple-element.14.table) | copy-start | bytes 69124
where the time goes:
time: 37.9 us; the launch traced here: 37.5 us
  starting transfers between devices  11.9 us (31%)
  blocking collectives  10.8 us (28%)
  Pallas kernels  6.89 us (18%)
  waiting for transfers between devices  5.9 us (16%)
  local copies, waits for them, and re-layouts  1.24 us (3%)
  between operations  0.74 us (2%)
    all_to_all x1, blocking collectives, by_blocks(): lax.all_to_all(jnp.concatenate([grad_lat, jnp.broadcast_to(share[None], (...  10.8 us
    ppermute x1, starting transfers between devices, by_blocks(): lax.ppermute(arrived[1], 'space', [(c, c ^ 1) for c in range(parts)])  5.92 us
    all_to_all x1, starting transfers between devices, by_blocks(): pieces = lax.all_to_all(sent, 'space', 0, 0, tiled=True)  5.31 us
    all_to_all x1, waiting for transfers between devices, by_blocks(): pieces = lax.all_to_all(sent, 'space', 0, 0, tiled=True)  5.03 us
    pallas_call x1, Pallas kernels, by_blocks(): pl.pallas_call(forward_lon_kernel, out_shape=(jax.ShapeDtypeStruct((parts...  3.57 us
    pallas_call x1, Pallas kernels, by_blocks(): pl.pallas_call(functools.partial(inverse_lon_kernel, ortho_scale=ortho_sc...  2.24 us
    unnamed x14, local copies, waits for them, and re-layouts  1.19 us
    pallas_call x1, Pallas kernels, by_blocks(): pl.pallas_call(functools.partial(spectral_kernel, ortho_scale=ortho_scale...  1.08 us
  transfers between devices with their start and end apart: 3, of which 2 were waited for; matrix products, arithmetic and copies ran while one was open for 1% of the time, Pallas kernels for 0%

commit v1 on v0

--- a/solution.py
+++ b/solution.py
@@ -19,7 +19,7 @@
 LANES = 128
 THIRD = LANES - BS
 VMEM_LIMIT = 32 * 1024 * 1024
-WHOLE_VMEM = 60 * 1024 * 1024
+WHOLE_VMEM = 64 * 1024 * 1024 - 320 * 1024
 
 
 def shift_of(group):
@@ -75,24 +75,24 @@
     columns = [slice(k * LANES, (k + 1) * LANES) for k in range(tiles)]
     keep_copy = pltpu.make_async_copy(keep_hbm, keep, sems.at[0])
     keep_copy.start()
-    field_copies, mask_copies = [], []
-    for t, source in enumerate((act_hbm, cot_hbm)):
-        for k in range(tiles):
-            copy = pltpu.make_async_copy(
-                source.at[:, :, columns[k]], field.at[t, k], sems.at[1 + t * tiles + k]
-            )
-            copy.start()
-            field_copies.append(copy)
+    mask_copies, field_copies = [], []
     for t, source in enumerate((relu_hbm, shrink_hbm)):
         for p in range(2):
             for k in range(tiles):
                 copy = pltpu.make_async_copy(
                     source.at[:, p, :, columns[k]],
                     masks.at[t, p, k],
-                    sems.at[1 + (2 + 2 * t + p) * tiles + k],
+                    sems.at[1 + (2 * t + p) * tiles + k],
                 )
                 copy.start()
                 mask_copies.append(copy)
+    for t, source in enumerate((act_hbm, cot_hbm)):
+        for k in range(tiles):
+            copy = pltpu.make_async_copy(
+                source.at[:, :, columns[k]], field.at[t, k], sems.at[1 + (4 + t) * tiles + k]
+            )
+            copy.start()
+            field_copies.append(copy)
 
     keep_copy.wait()
     shape = (rows * 2 * kept, LON * rows)
@@ -130,22 +130,22 @@
 
     passed = gate(0, 1.0)
     scaled = gate(1, scale)
-
-    lines = []
+    per = table.shape[0]
+    owners = [owner_of(group, b) for b in range(BLOCKS)]
+    for b in range(BLOCKS):
+        out[owners[b], 2 * per :, 0:BS] = passed[:, b * BS : (b + 1) * BS]
+        beside = [scaled[:, b * BS + g * THIRD : b * BS + (g + 1) * THIRD] for g in range(3)]
+        out[owners[b], :, BS:] = jnp.concatenate(beside, axis=0)
+
     for t in range(2):
-        found = []
-        for k in range(0, tiles, 2):
-            for i in range(2):
-                field_copies[t * tiles + k + i].wait()
-            wide = jnp.concatenate(
-                [field.at[t, k + i].reshape(LON * rows, LANES)[...] for i in range(2)], axis=1
-            )
-            found.append(dot(table, wide, 1, 0).astype(BF))
-        lines.append(jnp.concatenate(found, axis=1))
-
-    packed = jnp.concatenate(lines + [passed, scaled], axis=0)
-    for b in range(BLOCKS):
-        out[owner_of(group, b)] = fold(packed[:, b * BS : (b + 1) * BS])
+        for copy in field_copies[t * tiles : (t + 1) * tiles]:
+            copy.wait()
+        wide = jnp.concatenate(
+            [field.at[t, k].reshape(LON * rows, LANES)[...] for k in range(tiles)], axis=1
+        )
+        lines = dot(table, wide, 1, 0).astype(BF)
+        for b in range(BLOCKS):
+            out[owners[b], t * per : (t + 1) * per, 0:BS] = lines[:, b * BS : (b + 1) * BS]
 
 
 def spectral_kernel(
@@ -211,20 +211,17 @@
     def turned(array):
         return jnp.concatenate([array[half:], -array[:half]], axis=0)
 
-    at = 2 * BS * 3 // 4
+    at = 3 * BS // 4
+    blank = jnp.zeros((terms.shape[2] - at - 1, LANES), F32)
     for a, (left, right) in enumerate(((spec_act, grad_pre), (hidden, grad_out))):
         slot = (a + device) % 2
-        matrices = jnp.concatenate(
-            [dot(left, right, 0, 0), dot(left, turned(right), 0, 0)], axis=0
-        )
-        terms[slot, 0:at, :] = fold(matrices).astype(BF)
         wide = right.astype(F32)
-        sums = [jnp.sum(wide[p * half : (p + 1) * half], axis=0, keepdims=True) for p in range(2)]
-        rest = terms.shape[1] - at
-        sums = jnp.concatenate(sums + [jnp.zeros((rest - 2, BS), F32)], axis=0)
-        terms[slot, at:, :] = jnp.concatenate(
-            [sums, jnp.zeros((rest, THIRD), F32)], axis=1
-        ).astype(BF)
+        for p, other in enumerate((right, turned(right))):
+            summed = jnp.sum(wide[p * half : (p + 1) * half], axis=0, keepdims=True)
+            summed = jnp.concatenate([summed, jnp.zeros((1, THIRD), F32)], axis=1)
+            terms[slot, p] = jnp.concatenate(
+                [fold(dot(left, other, 0, 0)), summed, blank], axis=0
+            ).astype(BF)
 
     grad_spec = adjoint(grad_pre, first).astype(BF)
     lines = dot(lat_t[...], grad_spec, 1, 0)
@@ -232,27 +229,11 @@
     grad_lat[...] = lines.reshape(grad_lat.shape)
 
 
-def inverse_lon_kernel(
-    table,
-    pieces,
-    field_hbm,
-    first_hbm,
-    second_hbm,
-    bias_first,
-    bias_second,
-    lines,
-    field,
-    matrices,
-    sems,
-    *,
-    ortho_scale,
-    grad_norm,
-):
+def inverse_lon_kernel(table, pieces, field_hbm, lines, field, sems, *, ortho_scale):
     rows = field_hbm.shape[1]
     per = table.shape[0]
     tiles = C // LANES
     group = lax.axis_index("dp")
-    matrix_rows = 2 * BS * 3 // 4
     copies = []
     for b in range(BLOCKS):
         lines[:, b * BS : (b + 1) * BS] = pieces[owner_of(group, b), 0:per, 0:BS]
@@ -269,21 +250,23 @@
             )
             copy.start()
             copies.append(copy)
-    for a, (target, vector) in enumerate(((first_hbm, bias_first), (second_hbm, bias_second))):
-        for k in range(2):
-            sources = [pieces[4 * y + 2 * k + a, per:, :].astype(F32) for y in range(2)]
-            total = (sources[0] + sources[1]) * grad_norm
-            opened = unfold(total[:matrix_rows])
-            for p in range(2):
-                matrices[a, p, k * BS : (k + 1) * BS, :] = opened[p * BS : (p + 1) * BS]
-                vector[p : p + 1, k * BS : (k + 1) * BS] = total[
-                    matrix_rows + p : matrix_rows + p + 1, :BS
-                ]
-        copy = pltpu.make_async_copy(matrices.at[a], target, sems.at[tiles + a])
-        copy.start()
-        copies.append(copy)
     for copy in copies:
         copy.wait()
+
+
+def gathered_kernel(pieces, others, first, second, bias_first, bias_second, *, grad_norm):
+    core = lax.axis_index("space") % 2
+    per = pieces.shape[1] - others.shape[1]
+    at = 3 * BS // 4
+    for a, (target, vector) in enumerate(((first, bias_first), (second, bias_second))):
+        for k in range(2):
+            near, far = 2 * k + a, 4 + 2 * k + a
+            own = pieces[near, per:, :].astype(F32) + pieces[far, per:, :].astype(F32)
+            other = others[near].astype(F32) + others[far].astype(F32)
+            for p in range(2):
+                total = jnp.where(core == p, own, other) * grad_norm
+                target[p, k * BS : (k + 1) * BS, :] = unfold(total[:at])
+                vector[p : p + 1, k * BS : (k + 1) * BS] = total[at : at + 1, :BS]
 
 
 def whole(memory=pltpu.VMEM):
@@ -304,7 +287,7 @@
     tiles = C // LANES
     per = rows * 2 * kept
     height = (2 * per + 4 * lat_len) * 3 // 4
-    term_rows = 2 * BS * 3 // 4 + 16
+    term_rows = 3 * BS // 4 + 8
 
     sent, table = pl.pallas_call(
         forward_lon_kernel,
@@ -336,7 +319,7 @@
         functools.partial(spectral_kernel, ortho_scale=ortho_scale, rows=rows, kept=kept),
         out_shape=(
             jax.ShapeDtypeStruct((parts, per, LANES), BF),
-            jax.ShapeDtypeStruct((2, term_rows, LANES), BF),
+            jax.ShapeDtypeStruct((2, 2, term_rows, LANES), BF),
         ),
         in_specs=[whole()] * 6,
         out_specs=(whole(), whole()),
@@ -355,37 +338,46 @@
     )
     other = lax.ppermute(arrived[1], "space", [(c, c ^ 1) for c in range(parts)])
     share = (arrived[0].astype(F32) + other.astype(F32)).astype(BF)
+    share = jnp.broadcast_to(share[None], (parts // 2,) + share.shape)
     returned = lax.all_to_all(
-        jnp.concatenate(
-            [grad_lat, jnp.broadcast_to(share[None], (parts,) + share.shape)], axis=1
-        ),
+        jnp.concatenate([grad_lat, share.reshape(parts, term_rows, LANES)], axis=1),
         "space",
         0,
         0,
         tiled=True,
     )
+    others = lax.ppermute(returned[:, per:, :], "space", [(c, c ^ 1) for c in range(parts)])
 
     keep_rows = C // groups
-    field, first, second, bias_first, bias_second = pl.pallas_call(
-        functools.partial(inverse_lon_kernel, ortho_scale=ortho_scale, grad_norm=grad_norm),
+    field = pl.pallas_call(
+        functools.partial(inverse_lon_kernel, ortho_scale=ortho_scale),
+        out_shape=jax.ShapeDtypeStruct((LON, rows, C), BF),
+        in_specs=[whole(), whole()],
+        out_specs=whole(pl.ANY),
+        scratch_shapes=[
+            pltpu.VMEM((per, C), BF),
+            pltpu.VMEM((tiles, LON, rows, LANES), BF),
+            pltpu.SemaphoreType.DMA((tiles,)),
+        ],
+        compiler_params=params,
+        cost_estimate=pl.CostEstimate(
+            flops=2 * per * LON * rows * C, bytes_accessed=8 * LON * rows * C, transcendentals=0
+        ),
+        name="inverse_lon",
+    )(table, returned)
+    first, second, bias_first, bias_second = pl.pallas_call(
+        functools.partial(gathered_kernel, grad_norm=grad_norm),
         out_shape=(
-            jax.ShapeDtypeStruct((LON, rows, C), BF),
             jax.ShapeDtypeStruct((2, keep_rows, BS), F32),
             jax.ShapeDtypeStruct((2, keep_rows, BS), F32),
             jax.ShapeDtypeStruct((2, keep_rows), F32),
             jax.ShapeDtypeStruct((2, keep_rows), F32),
         ),
         in_specs=[whole(), whole()],
-        out_specs=(whole(pl.ANY),) * 3 + (whole(),) * 2,
-        scratch_shapes=[
-            pltpu.VMEM((per, C), BF),
-            pltpu.VMEM((tiles, LON, rows, LANES), BF),
-            pltpu.VMEM((2, 2, keep_rows, BS), F32),
-            pltpu.SemaphoreType.DMA((tiles + 2,)),
-        ],
+        out_specs=(whole(),) * 4,
         compiler_params=params,
-        name="inverse_lon",
-    )(table, returned)
+        name="gathered",
+    )(returned, others)
     return field.transpose(1, 0, 2)[None], first, second, bias_first, bias_second
 
 

time: 37.9 us -> 36.6 us (0.966)
  blocking collectives: 10.8 us -> 9.02 us
  local copies, waits for them, and re-layouts: 1.24 us -> 1.87 us
    all_to_all x1, blocking collectives: 10.8 us -> 9.02 us  [by_blocks(): lax.all_to_all(jnp.concatenate([grad_lat, share.reshape(parts, term_rows,...]
    pallas_call x0 -> x1, Pallas kernels: none -> 0.87 us  [by_blocks(): pl.pallas_call(functools.partial(gathered_kernel, grad_norm=grad_norm), o...]
    pallas_call x1, Pallas kernels: 2.24 us -> 1.47 us  [by_blocks(): pl.pallas_call(functools.partial(inverse_lon_kernel, ortho_scale=ortho_sc...]
    unnamed x14, local copies, waits for them, and re-layouts: 1.19 us -> 1.83 us
  transfers between devices with their start and end apart: 3 -> 4, of which waited for: 2 -> 2; matrix products, arithmetic and copies ran while one was open for 1% -> 1% of each run, Pallas kernels for 0% -> 4%
where the time goes in v1:
time: 36.6 us; the launch traced here: 36.2 us
  starting transfers between devices  12 us (33%)
  blocking collectives  9.02 us (25%)
  Pallas kernels  6.62 us (18%)
  waiting for transfers between devices  5.91 us (16%)
  local copies, waits for them, and re-layouts  1.87 us (5%)
  between operations  0.76 us (2%)
    all_to_all x1, blocking collectives, by_blocks(): lax.all_to_all(jnp.concatenate([grad_lat, share.reshape(parts, term_rows,...  9.02 us
    ppermute x1, starting transfers between devices, by_blocks(): lax.ppermute(arrived[1], 'space', [(c, c ^ 1) for c in range(parts)])  5.92 us
    all_to_all x1, starting transfers between devices, by_blocks(): pieces = lax.all_to_all(sent, 'space', 0, 0, tiled=True)  5.31 us
    all_to_all x1, waiting for transfers between devices, by_blocks(): pieces = lax.all_to_all(sent, 'space', 0, 0, tiled=True)  5.03 us
    pallas_call x1, Pallas kernels, by_blocks(): pl.pallas_call(forward_lon_kernel, out_shape=(jax.ShapeDtypeStruct((parts...  3.2 us
    unnamed x14, local copies, waits for them, and re-layouts  1.83 us
    pallas_call x1, Pallas kernels, by_blocks(): pl.pallas_call(functools.partial(inverse_lon_kernel, ortho_scale=ortho_sc...  1.47 us
    pallas_call x1, Pallas kernels, by_blocks(): pl.pallas_call(functools.partial(spectral_kernel, ortho_scale=ortho_scale...  1.08 us
  transfers between devices with their start and end apart: 4, of which 2 were waited for; matrix products, arithmetic and copies ran while one was open for 1% of the time, Pallas kernels for 4%

profile of v1, /device:TPU:0, one launch (start us, length us, event | category | flops | bytes accessed | tf_op | source)
XLA Modules:
  0.0 36.2 jit_solution(8622977475026993415)
XLA Ops:
  0.6 3.2 %forward_lon.1 = (bf16[8,96,128]{2,1,0:T(8,128)(2,1)}, bf16[32,360]{1,0:T(8,128)(2,1)}) custom-call(s32[8]{0:T(128)} %keep_hbm.1, bf16[180,2,768]{2,1,0:T(2,128)(2,1)} %bitcast.21, bf16[180,2,768]{2,1,0:T(2,128)(2,1)} %bitcast.22, s32[16,2,1,768]{3,2,1,0:T(1,128)} %bitcast.23, s32[16,2,1,768]{3,2,1,0:T(1,128)} %bitcast.24), custom_call_target="tpu_custom_call" | custom-call | tf_op jit(solution)/shard_map/forward_lon/pallas_call | solution.py:292
  3.8 0.0 copy-start.4
  3.9 5.3 %all-to-all-start = ((bf16[8,96,128]{2,1,0:T(8,128)(2,1)}), bf16[8,96,128]{2,1,0:T(8,128)(2,1)S(1)}, u32[]{:S(2)}, u32[]{:S(2)}) async-start(bf16[8,96,128]{2,1,0:T(8,128)(2,1)} %get-tuple-element.14), calls=%async_computation | async-start | bytes 393216 | tf_op jit(solution)/shard_map/all_to_all | solution.py:315
  9.2 0.0 copy-done.4
  9.2 0.0 copy-start.5
  9.2 0.2 copy.15.first_all
  9.4 0.7 %copy-done.5 = bf16[2,768,96]{1,2,0:T(8,128)(2,1)S(1)} copy-done((bf16[2,768,96]{1,2,0:T(8,128)(2,1)S(1)}, bf16[2,768,96]{1,2,0:T(8,128)(2,1)}, u32[]{:S(2)}) %copy-start.5) | copy-done | bytes 294936
  10.1 0.0 copy-start
  10.1 0.2 copy.16.second_all
  10.4 5.0 %all-to-all-done.pieces = bf16[8,96,128]{2,1,0:T(8,128)(2,1)S(1)} async-done(((bf16[8,96,128]{2,1,0:T(8,128)(2,1)}), bf16[8,96,128]{2,1,0:T(8,128)(2,1)S(1)}, u32[]{:S(2)}, u32[]{:S(2)}) %all-to-all-start) | async-done | bytes 196640 | tf_op jit(solution)/shard_map/all_to_all | solution.py:315
  15.4 0.0 copy-done
  15.4 0.0 copy-done.1
  15.4 0.0 copy-done.3
  15.4 1.1 %spectral.1 = (bf16[8,32,128]{2,1,0:T(8,128)(2,1)S(1)}, bf16[2,2,80,128]{3,2,1,0:T(8,128)(2,1)S(1)}) custom-call(bf16[8,96,128]{2,1,0:T(8,128)(2,1)S(1)} %all-to-all-done.pieces, bf16[2,768,96]{2,1,0:T(8,128)(2,1)S(1)} %copy.15.first_all, bf16[2,768,96]{2,1,0:T(8,128)(2,1)S(1)} %copy.16.second_all, f32[2,768]{1,0:T(2,128)S(1)} %copy-done.3, ...), custom_call_target="tpu_custom_call" | custom-call | tf_op jit(solution)/shard_map/spectral/pallas_call | solution.py:318
  16.5 0.7 %collective-permute-start = (bf16[2,2,80,128]{3,2,1,0:T(8,128)(2,1)S(1)}, bf16[2,2,80,128]{3,2,1,0:T(8,128)(2,1)S(1)}, u32[]{:S(2)}, u32[]{:S(2)}) collective-permute-start(bf16[2,2,80,128]{3,2,1,0:T(8,128)(2,1)S(1)} %get-tuple-element.16), channel_id=1, source_target_pairs={{0,0},{1,9},{2,2},{3,11},{4,20},{5,29},{6,22},{7,31},{8,16},{9,25}... | collective-permute-start | bytes 245768 | tf_op jit(solution)/shard_map/ppermute | solution.py:330
  17.2 0.0 collective-permute-done
  17.2 5.9 %collective-permute-start.1 = (bf16[2,80,128]{2,1,0:T(8,128)(2,1)S(1)}, bf16[2,80,128]{2,1,0:T(8,128)(2,1)S(1)}, u32[]{:S(2)}, u32[]{:S(2)}) collective-permute-start(bf16[2,80,128]{2,1,0:T(8,128)(2,1)S(1)} %slice_bitcast_fusion), channel_id=1, source_target_pairs={{0,1},{1,0},{2,3},{3,2},{4,5},{5,4},{6,7},{7,6},{8,9},{9,8},{10,11... | collective-permute-start | bytes 122888 | tf_op jit(solution)/shard_map/ppermute | solution.py:339
  23.1 0.9 %collective-permute-done.1 = bf16[2,80,128]{2,1,0:T(8,128)(2,1)S(1)} collective-permute-done((bf16[2,80,128]{2,1,0:T(8,128)(2,1)S(1)}, bf16[2,80,128]{2,1,0:T(8,128)(2,1)S(1)}, u32[]{:S(2)}, u32[]{:S(2)}) %collective-permute-start.1) | collective-permute-done | bytes 40992 | tf_op jit(solution)/shard_map/ppermute | solution.py:339
  24.1 9.0 %all_to_all.10.pieces = bf16[8,112,128]{2,1,0:T(8,128)(2,1)S(1)} all-to-all(bf16[8,112,128]{2,1,0:T(8,128)(2,1)S(1)} %pad_maximum_fusion), channel_id=1, replica_groups=mesh['dp'=4,'space'=8] {'space'}, dimensions={0} | all-to-all | bytes 458752 | tf_op jit(solution)/shard_map/all_to_all | solution.py:342
  33.1 0.1 collective-permute-start.2
  33.2 0.6 %copy-done.2 = bf16[32,360]{1,0:T(8,128)(2,1)S(1)} copy-done((bf16[32,360]{1,0:T(8,128)(2,1)S(1)}, bf16[32,360]{1,0:T(8,128)(2,1)}, u32[]{:S(2)}) %copy-start.2) | copy-done | bytes 23064
  33.8 1.5 %inverse_lon.1 = bf16[180,2,768]{2,1,0:T(2,128)(2,1)} custom-call(bf16[32,360]{1,0:T(8,128)(2,1)S(1)} %copy-done.2, bf16[8,112,128]{2,1,0:T(8,128)(2,1)S(1)} %all_to_all.10.pieces), custom_call_target="tpu_custom_call" | custom-call | flops 17694720 | bytes 2211840 | tf_op jit(solution)/shard_map/inverse_lon/pallas_call | solution.py:352
  35.3 0.0 collective-permute-done.2.others
  35.3 0.9 %gathered.1 = (f32[2,192,96]{2,1,0:T(8,128)}, f32[2,192,96]{2,1,0:T(8,128)}, f32[2,192]{1,0:T(2,128)}, f32[2,192]{1,0:T(2,128)}) custom-call(bf16[8,112,128]{2,1,0:T(8,128)(2,1)S(1)} %all_to_all.10.pieces, bf16[8,80,128]{2,1,0:T(8,128)(2,1)S(1)} %collective-permute-done.2.others), custom_call_target="tpu_custom_call" | custom-call | tf_op jit(solution)/shard_map/gathered/pallas_call | solution.py:368
  (8 shorter events, 0.1 us)
Async XLA Ops:
  3.8 5.3 %copy-start.4 = (bf16[2,768,96]{1,2,0:T(8,128)(2,1)S(1)}, bf16[2,768,96]{1,2,0:T(8,128)(2,1)}, u32[]{:S(2)}) copy-start(bf16[2,768,96]{1,2,0:T(8,128)(2,1)} %param.12) | copy-start | bytes 884740
  3.9 11.5 %all-to-all-start = ((bf16[8,96,128]{2,1,0:T(8,128)(2,1)}), bf16[8,96,128]{2,1,0:T(8,128)(2,1)S(1)}, u32[]{:S(2)}, u32[]{:S(2)}) async-start(bf16[8,96,128]{2,1,0:T(8,128)(2,1)} %get-tuple-element.14), calls=%async_computation | async-start | bytes 393216 | tf_op jit(solution)/shard_map/all_to_all | solution.py:315
  9.2 1.0 %copy-start.5 = (bf16[2,768,96]{1,2,0:T(8,128)(2,1)S(1)}, bf16[2,768,96]{1,2,0:T(8,128)(2,1)}, u32[]{:S(2)}) copy-start(bf16[2,768,96]{1,2,0:T(8,128)(2,1)} %param.13) | copy-start | bytes 884740
  10.1 5.3 %copy-start = (bf16[256,256]{1,0:T(8,128)(2,1)S(1)}, bf16[256,256]{1,0:T(8,128)(2,1)}, u32[]{:S(2)}) copy-start(bf16[256,256]{1,0:T(8,128)(2,1)} %constant.5.clone.lat_t) | copy-start | bytes 393220
  10.1 5.3 %copy-start.1 = (bf16[256,256]{1,0:T(8,128)(2,1)S(1)}, bf16[256,256]{1,0:T(8,128)(2,1)}, u32[]{:S(2)}) copy-start(bf16[256,256]{1,0:T(8,128)(2,1)} %constant.4.clone.lat) | copy-start | bytes 393220
  10.1 5.3 %copy-start.3 = (f32[2,768]{1,0:T(2,128)S(1)}, f32[2,768]{1,0:T(2,128)}, u32[]{:S(2)}) copy-start(f32[2,768]{1,0:T(2,128)} %bias.1) | copy-start | bytes 18436
  16.5 0.7 %collective-permute-start = (bf16[2,2,80,128]{3,2,1,0:T(8,128)(2,1)S(1)}, bf16[2,2,80,128]{3,2,1,0:T(8,128)(2,1)S(1)}, u32[]{:S(2)}, u32[]{:S(2)}) collective-permute-start(bf16[2,2,80,128]{3,2,1,0:T(8,128)(2,1)S(1)} %get-tuple-element.16), channel_id=1, source_target_pairs={{0,0},{1,9},{2,2},{3,11},{4,20},{5,29},{6,22},{7,31},{8,16},{9,25}... | collective-permute-start | bytes 245768 | tf_op jit(solution)/shard_map/ppermute | solution.py:330
  17.2 6.8 %collective-permute-start.1 = (bf16[2,80,128]{2,1,0:T(8,128)(2,1)S(1)}, bf16[2,80,128]{2,1,0:T(8,128)(2,1)S(1)}, u32[]{:S(2)}, u32[]{:S(2)}) collective-permute-start(bf16[2,80,128]{2,1,0:T(8,128)(2,1)S(1)} %slice_bitcast_fusion), channel_id=1, source_target_pairs={{0,1},{1,0},{2,3},{3,2},{4,5},{5,4},{6,7},{7,6},{8,9},{9,8},{10,11... | collective-permute-start | bytes 122888 | tf_op jit(solution)/shard_map/ppermute | solution.py:339
  33.1 0.7 %copy-start.2 = (bf16[32,360]{1,0:T(8,128)(2,1)S(1)}, bf16[32,360]{1,0:T(8,128)(2,1)}, u32[]{:S(2)}) copy-start(bf16[32,360]{1,0:T(8,128)(2,1)} %get-tuple-element.13.table) | copy-start | bytes 69124
  33.1 2.2 %collective-permute-start.2 = (bf16[8,80,128]{2,1,0:T(8,128)(2,1)S(1)}, bf16[8,80,128]{2,1,0:T(8,128)(2,1)S(1)}, u32[]{:S(2)}, u32[]{:S(2)}) collective-permute-start(bf16[8,80,128]{2,1,0:T(8,128)(2,1)S(1)} %slice.14), channel_id=1, source_target_pairs={{0,1},{1,0},{2,3},{3,2},{4,5},{5,4},{6,7},{7,6},{8,9},{9,8},{10,11... | collective-permute-start | bytes 491528 | tf_op jit(solution)/shard_map/ppermute | solution.py:349

commit v2 on v1

--- a/solution.py
+++ b/solution.py
@@ -19,7 +19,6 @@
 LANES = 128
 THIRD = LANES - BS
 VMEM_LIMIT = 32 * 1024 * 1024
-WHOLE_VMEM = 64 * 1024 * 1024 - 320 * 1024
 
 
 def shift_of(group):
@@ -65,9 +64,23 @@
     return jnp.concatenate([array[:, :BS], jnp.concatenate(beside, axis=1)], axis=0)
 
 
+def window_of(block):
+    tile = jnp.minimum(block * BS // LANES, C // LANES - 2)
+    return pl.multiple_of(tile * LANES, LANES), block * BS - tile * LANES
+
+
 def forward_lon_kernel(
-    keep_hbm, act_hbm, cot_hbm, relu_hbm, shrink_hbm, out, table_out, field, masks, keep, sems
+    keep_hbm,
+    act_hbm,
+    cot_hbm,
+    relu_hbm,
+    shrink_hbm,
+    *refs,
 ):
+    weights_hbm, matrices_hbm, refs = refs[:3], refs[3:5], refs[5:]
+    out, table_out, *fetched, field, masks, keep, sems = refs
+    group, device = lax.axis_index("dp"), lax.axis_index("space")
+    start, _ = window_of(block_of(group, device))
     kept = keep.shape[0]
     rows = act_hbm.shape[1]
     modes = relu_hbm.shape[0]
@@ -93,6 +106,15 @@
             )
             copy.start()
             field_copies.append(copy)
+    sources = [
+        source.at[(slice(None),) * (len(source.shape) - 1) + (pl.ds(start, 2 * LANES),)]
+        for source in weights_hbm
+    ] + list(matrices_hbm)
+    other_copies = []
+    for i, (source, target) in enumerate(zip(sources, fetched)):
+        copy = pltpu.make_async_copy(source, target, sems.at[1 + 6 * tiles + i])
+        copy.start()
+        other_copies.append(copy)
 
     keep_copy.wait()
     shape = (rows * 2 * kept, LON * rows)
@@ -107,8 +129,7 @@
     table = jnp.where(line // (2 * kept) == column % rows, table, 0.0).astype(BF)
     table_out[...] = table
 
-    group = lax.axis_index("dp")
-    own = keep[lax.axis_index("space")]
+    own = keep[device]
     scale = jnp.where((own == 0) | (2 * own == LON), 1.0, 2.0)
     for copy in mask_copies:
         copy.wait()
@@ -146,20 +167,26 @@
         lines = dot(table, wide, 1, 0).astype(BF)
         for b in range(BLOCKS):
             out[owners[b], t * per : (t + 1) * per, 0:BS] = lines[:, b * BS : (b + 1) * BS]
+    for copy in other_copies:
+        copy.wait()
 
 
 def spectral_kernel(
-    pieces, first_all, second_all, bias, lat, lat_t, grad_lat, terms, *, ortho_scale, rows, kept
+    pieces, first_wide, second_wide, bias_wide, lat, lat_t, grad_lat, terms, *, ortho_scale, rows, kept
 ):
     device = lax.axis_index("space")
-    block = block_of(lax.axis_index("dp"), device)
+    _, offset = window_of(block_of(lax.axis_index("dp"), device))
     parts = pieces.shape[0]
     per = rows * 2 * kept
     half = parts * per // 2
     modes = half // kept
-    place = pl.ds(pl.multiple_of(block * BS, BS), BS)
-    first = [first_all[p, place, :] for p in range(2)]
-    second = [second_all[p, place, :] for p in range(2)]
+    chosen = lax.broadcasted_iota(jnp.int32, (2 * LANES, BS), 0) == (
+        lax.broadcasted_iota(jnp.int32, (2 * LANES, BS), 1) + offset
+    )
+    chosen = jnp.where(chosen, 1.0, 0.0).astype(BF)
+    first = [dot(first_wide[p], chosen, 1, 0).astype(BF) for p in range(2)]
+    second = [dot(second_wide[p], chosen, 1, 0).astype(BF) for p in range(2)]
+    bias = pltpu.roll(bias_wide[...], (2 * LANES - offset) % (2 * LANES), 1)
     opened = [unfold(pieces[i]) for i in range(parts)]
 
     def spectrum(t):
@@ -183,27 +210,20 @@
     weight = mask(1)
     grad_out = jnp.where(weight > 0.0, weight * spec_cot.astype(F32), 0.0).astype(BF)
 
-    bias_real = jnp.zeros((1, BS), F32)
-    bias_imag = jnp.zeros((1, BS), F32)
-    for b in range(BLOCKS):
-        mine = block == b
-        bias_real = jnp.where(mine, bias[0:1, b * BS : (b + 1) * BS], bias_real)
-        bias_imag = jnp.where(mine, bias[1:2, b * BS : (b + 1) * BS], bias_imag)
-
-    by_real = dot(spec_act, first[0], 1, 0)
-    by_imag = dot(spec_act, first[1], 1, 0)
+    by_real = dot(spec_act, first[0], 1, 1)
+    by_imag = dot(spec_act, first[1], 1, 1)
     pre = jnp.concatenate(
         [
-            by_real[:half] - by_imag[half:] + bias_real,
-            by_imag[:half] + by_real[half:] + bias_imag,
+            by_real[:half] - by_imag[half:] + bias[0:1, :BS],
+            by_imag[:half] + by_real[half:] + bias[1:2, :BS],
         ],
         axis=0,
     )
     hidden = jnp.where(passed, pre, 0.0).astype(BF)
 
     def adjoint(operand, matrix):
-        real = dot(operand, matrix[0], 1, 1)
-        imag = dot(operand, matrix[1], 1, 1)
+        real = dot(operand, matrix[0], 1, 0)
+        imag = dot(operand, matrix[1], 1, 0)
         return jnp.concatenate([real[:half] + imag[half:], real[half:] - imag[:half]], axis=0)
 
     grad_pre = jnp.where(passed, adjoint(grad_out, second), 0.0).astype(BF)
@@ -289,32 +309,47 @@
     height = (2 * per + 4 * lat_len) * 3 // 4
     term_rows = 3 * BS // 4 + 8
 
-    sent, table = pl.pallas_call(
+    lat = latitude_matrix(lat_len, kept)
+    sent, table, *fetched = pl.pallas_call(
         forward_lon_kernel,
         out_shape=(
-            jax.ShapeDtypeStruct((parts, height, LANES), BF),
-            jax.ShapeDtypeStruct((per, LON * rows), BF),
+            pltpu.VMEM((parts, height, LANES), BF),
+            pltpu.VMEM((per, LON * rows), BF),
+            pltpu.VMEM((2, BS, 2 * LANES), BF),
+            pltpu.VMEM((2, BS, 2 * LANES), BF),
+            pltpu.VMEM((2, 2 * LANES), F32),
+            pltpu.VMEM(lat.shape, BF),
+            pltpu.VMEM(lat.shape, BF),
         ),
-        in_specs=[whole(pl.ANY)] * 5,
-        out_specs=(whole(), whole()),
+        in_specs=[whole(pl.ANY)] * 10,
+        out_specs=(whole(),) * 7,
         scratch_shapes=[
             pltpu.VMEM((2, tiles, LON, rows, LANES), BF),
             pltpu.VMEM((2, 2, tiles, lat_len, 1, LANES), jnp.int32),
             pltpu.SMEM((kept,), jnp.int32),
-            pltpu.SemaphoreType.DMA((1 + 6 * tiles,)),
+            pltpu.SemaphoreType.DMA((6 + 6 * tiles,)),
         ],
-        compiler_params=pltpu.CompilerParams(vmem_limit_bytes=WHOLE_VMEM),
+        compiler_params=params,
         name="forward_lon",
     )(
-        lon_keep,
-        activations[0].transpose(1, 0, 2),
-        cotangent[0].transpose(1, 0, 2),
-        relu_mask[0],
-        shrink_mask[0],
+        *(
+            pltpu.with_memory_space_constraint(array, pltpu.HBM)
+            for array in (
+                lon_keep,
+                activations[0].transpose(1, 0, 2),
+                cotangent[0].transpose(1, 0, 2),
+                relu_mask[0],
+                shrink_mask[0],
+                w_first.transpose(0, 2, 1),
+                w_second.transpose(0, 2, 1),
+                b_first,
+                jnp.asarray(lat, BF),
+                jnp.asarray(lat.T, BF),
+            )
+        )
     )
     pieces = lax.all_to_all(sent, "space", 0, 0, tiled=True)
 
-    lat = latitude_matrix(lat_len, kept)
     grad_lat, terms = pl.pallas_call(
         functools.partial(spectral_kernel, ortho_scale=ortho_scale, rows=rows, kept=kept),
         out_shape=(
@@ -325,7 +360,7 @@
         out_specs=(whole(), whole()),
         compiler_params=params,
         name="spectral",
-    )(pieces, w_first, w_second, b_first, jnp.asarray(lat, BF), jnp.asarray(lat.T, BF))
+    )(pieces, *fetched)
 
     arrived = lax.ppermute(
         terms,

time: 36.6 us -> 34.7 us (0.948)
  blocking collectives: 9.02 us -> 20.2 us
  starting transfers between devices: 12 us -> 6.65 us
  waiting for transfers between devices: 5.91 us -> 0.88 us
  local copies, waits for them, and re-layouts: 1.87 us -> 0.04 us
  Pallas kernels: 6.62 us -> 5.89 us
    all_to_all x0 -> x1, blocking collectives: none -> 11.2 us  [by_blocks(): pieces = lax.all_to_all(sent, 'space', 0, 0, tiled=True)]
    all_to_all x1 -> x0, starting transfers between devices: 5.31 us -> none  [by_blocks(): pieces = lax.all_to_all(sent, 'space', 0, 0, tiled=True)]
    all_to_all x1 -> x0, waiting for transfers between devices: 5.03 us -> none  [by_blocks(): pieces = lax.all_to_all(sent, 'space', 0, 0, tiled=True)]
    unnamed x14 -> x0, local copies, waits for them, and re-layouts: 1.83 us -> none
    pallas_call x1, Pallas kernels: 3.2 us -> 2.58 us  [by_blocks(): pl.pallas_call(forward_lon_kernel, out_shape=(pltpu.VMEM((parts, height,...]
  transfers between devices with their start and end apart: 4 -> 3, of which waited for: 2 -> 1; matrix products, arithmetic and copies ran while one was open for 1% -> 0% of each run, Pallas kernels for 4% -> 4%
where the time goes in v2:
time: 34.7 us; the launch traced here: 34.4 us
  blocking collectives  20.2 us (58%)
  starting transfers between devices  6.65 us (19%)
  Pallas kernels  5.89 us (17%)
  waiting for transfers between devices  0.88 us (3%)
  between operations  0.72 us (2%)
    all_to_all x1, blocking collectives, by_blocks(): pieces = lax.all_to_all(sent, 'space', 0, 0, tiled=True)  11.2 us
    all_to_all x1, blocking collectives, by_blocks(): lax.all_to_all(jnp.concatenate([grad_lat, share.reshape(parts, term_rows,...  9.01 us
    ppermute x1, starting transfers between devices, by_blocks(): lax.ppermute(arrived[1], 'space', [(c, c ^ 1) for c in range(parts)])  5.92 us
    pallas_call x1, Pallas kernels, by_blocks(): pl.pallas_call(forward_lon_kernel, out_shape=(pltpu.VMEM((parts, height,...  2.58 us
    pallas_call x1, Pallas kernels, by_blocks(): pl.pallas_call(functools.partial(inverse_lon_kernel, ortho_scale=ortho_sc...  1.51 us
    pallas_call x1, Pallas kernels, by_blocks(): pl.pallas_call(functools.partial(spectral_kernel, ortho_scale=ortho_scale...  0.92 us
    pallas_call x1, Pallas kernels, by_blocks(): pl.pallas_call(functools.partial(gathered_kernel, grad_norm=grad_norm), o...  0.88 us
    ppermute x1, waiting for transfers between devices, by_blocks(): lax.ppermute(arrived[1], 'space', [(c, c ^ 1) for c in range(parts)])  0.87 us
  transfers between devices with their start and end apart: 3, of which 1 were waited for; matrix products, arithmetic and copies ran while one was open for 0% of the time, Pallas kernels for 4%

profile of v2, /device:TPU:0, one launch (start us, length us, event | category | flops | bytes accessed | tf_op | source)
XLA Modules:
  0.0 34.4 jit_solution(1306205852074867506)
XLA Ops:
  0.6 2.6 %forward_lon.1 = (bf16[8,96,128]{2,1,0:T(8,128)(2,1)S(1)}, bf16[32,360]{1,0:T(8,128)(2,1)S(1)}, bf16[2,96,256]{2,1,0:T(8,128)(2,1)S(1)}, bf16[2,96,256]{2,1,0:T(...) custom-call(s32[8]{0:T(128)} %keep_hbm.1, ...), custom_call_target="tpu_custom_call" | custom-call | tf_op jit(solution)/shard_map/forward_lon/pallas_call | solution.py:313
  3.2 11.2 %all_to_all.10.pieces = bf16[8,96,128]{2,1,0:T(8,128)(2,1)S(1)} all-to-all(bf16[8,96,128]{2,1,0:T(8,128)(2,1)S(1)} %get-tuple-element.19), channel_id=1, replica_groups=mesh['dp'=4,'space'=8] {'space'}, dimensions={0} | all-to-all | bytes 393216 | tf_op jit(solution)/shard_map/all_to_all | solution.py:351
  14.4 0.9 %spectral.1 = (bf16[8,32,128]{2,1,0:T(8,128)(2,1)S(1)}, bf16[2,2,80,128]{3,2,1,0:T(8,128)(2,1)S(1)}) custom-call(bf16[8,96,128]{2,1,0:T(8,128)(2,1)S(1)} %all_to_all.10.pieces, bf16[2,96,256]{2,1,0:T(8,128)(2,1)S(1)} %get-tuple-element.20.first_wide, bf16[2,96,256]{2,1,0:T(8,128)(2,1)S(1)} %get-tuple-element.21.second_wide, ...), custom_call_target="tpu_custom_call" | custom-call | tf_op jit(solution)/shard_map/spectral/pallas_call | solution.py:353
  15.4 0.7 %collective-permute-start = (bf16[2,2,80,128]{3,2,1,0:T(8,128)(2,1)S(1)}, bf16[2,2,80,128]{3,2,1,0:T(8,128)(2,1)S(1)}, u32[]{:S(2)}, u32[]{:S(2)}) collective-permute-start(bf16[2,2,80,128]{3,2,1,0:T(8,128)(2,1)S(1)} %get-tuple-element.26), channel_id=1, source_target_pairs={{0,0},{1,9},{2,2},{3,11},{4,20},{5,29},{6,22},{7,31},{8,16},{9,25}... | collective-permute-start | bytes 245768 | tf_op jit(solution)/shard_map/ppermute | solution.py:365
  16.0 0.0 collective-permute-done
  16.0 5.9 %collective-permute-start.1 = (bf16[2,80,128]{2,1,0:T(8,128)(2,1)S(1)}, bf16[2,80,128]{2,1,0:T(8,128)(2,1)S(1)}, u32[]{:S(2)}, u32[]{:S(2)}) collective-permute-start(bf16[2,80,128]{2,1,0:T(8,128)(2,1)S(1)} %slice_bitcast_fusion), channel_id=1, source_target_pairs={{0,1},{1,0},{2,3},{3,2},{4,5},{5,4},{6,7},{7,6},{8,9},{9,8},{10,11... | collective-permute-start | bytes 122888 | tf_op jit(solution)/shard_map/ppermute | solution.py:374
  22.0 0.9 %collective-permute-done.1 = bf16[2,80,128]{2,1,0:T(8,128)(2,1)S(1)} collective-permute-done((bf16[2,80,128]{2,1,0:T(8,128)(2,1)S(1)}, bf16[2,80,128]{2,1,0:T(8,128)(2,1)S(1)}, u32[]{:S(2)}, u32[]{:S(2)}) %collective-permute-start.1) | collective-permute-done | bytes 40992 | tf_op jit(solution)/shard_map/ppermute | solution.py:374
  22.9 9.0 %all_to_all.11.pieces = bf16[8,112,128]{2,1,0:T(8,128)(2,1)S(1)} all-to-all(bf16[8,112,128]{2,1,0:T(8,128)(2,1)S(1)} %pad_maximum_fusion), channel_id=1, replica_groups=mesh['dp'=4,'space'=8] {'space'}, dimensions={0} | all-to-all | bytes 458752 | tf_op jit(solution)/shard_map/all_to_all | solution.py:377
  31.9 0.1 collective-permute-start.2
  32.0 1.5 %inverse_lon.1 = bf16[180,2,768]{2,1,0:T(2,128)(2,1)} custom-call(bf16[32,360]{1,0:T(8,128)(2,1)S(1)} %get-tuple-element.18.table, bf16[8,112,128]{2,1,0:T(8,128)(2,1)S(1)} %all_to_all.11.pieces), custom_call_target="tpu_custom_call" | custom-call | flops 17694720 | bytes 2211840 | tf_op jit(solution)/shard_map/inverse_lon/pallas_call | solution.py:387
  33.5 0.0 collective-permute-done.2.others
  33.5 0.9 %gathered.1 = (f32[2,192,96]{2,1,0:T(8,128)}, f32[2,192,96]{2,1,0:T(8,128)}, f32[2,192]{1,0:T(2,128)}, f32[2,192]{1,0:T(2,128)}) custom-call(bf16[8,112,128]{2,1,0:T(8,128)(2,1)S(1)} %all_to_all.11.pieces, bf16[8,80,128]{2,1,0:T(8,128)(2,1)S(1)} %collective-permute-done.2.others), custom_call_target="tpu_custom_call" | custom-call | tf_op jit(solution)/shard_map/gathered/pallas_call | solution.py:403
  (5 shorter events, 0.1 us)
Async XLA Ops:
  15.4 0.7 %collective-permute-start = (bf16[2,2,80,128]{3,2,1,0:T(8,128)(2,1)S(1)}, bf16[2,2,80,128]{3,2,1,0:T(8,128)(2,1)S(1)}, u32[]{:S(2)}, u32[]{:S(2)}) collective-permute-start(bf16[2,2,80,128]{3,2,1,0:T(8,128)(2,1)S(1)} %get-tuple-element.26), channel_id=1, source_target_pairs={{0,0},{1,9},{2,2},{3,11},{4,20},{5,29},{6,22},{7,31},{8,16},{9,25}... | collective-permute-start | bytes 245768 | tf_op jit(solution)/shard_map/ppermute | solution.py:365
  16.0 6.8 %collective-permute-start.1 = (bf16[2,80,128]{2,1,0:T(8,128)(2,1)S(1)}, bf16[2,80,128]{2,1,0:T(8,128)(2,1)S(1)}, u32[]{:S(2)}, u32[]{:S(2)}) collective-permute-start(bf16[2,80,128]{2,1,0:T(8,128)(2,1)S(1)} %slice_bitcast_fusion), channel_id=1, source_target_pairs={{0,1},{1,0},{2,3},{3,2},{4,5},{5,4},{6,7},{7,6},{8,9},{9,8},{10,11... | collective-permute-start | bytes 122888 | tf_op jit(solution)/shard_map/ppermute | solution.py:374
  31.9 1.6 %collective-permute-start.2 = (bf16[8,80,128]{2,1,0:T(8,128)(2,1)S(1)}, bf16[8,80,128]{2,1,0:T(8,128)(2,1)S(1)}, u32[]{:S(2)}, u32[]{:S(2)}) collective-permute-start(bf16[8,80,128]{2,1,0:T(8,128)(2,1)S(1)} %slice.14), channel_id=1, source_target_pairs={{0,1},{1,0},{2,3},{3,2},{4,5},{5,4},{6,7},{7,6},{8,9},{9,8},{10,11... | collective-permute-start | bytes 491528 | tf_op jit(solution)/shard_map/ppermute | solution.py:384
